TPU v7x, 256 devices: a whole 4x4x8 slice. The times are simulated.
256 devices in a mesh: seq: 32 (over z, y), ch: 8 (over x, core).
Axes of the slice: x: 4, y: 4, z: 8, core: 2. Of those that a mesh axis runs over, the one named last changes fastest.
Arguments:
- tokens: bfloat16 [8192, 8192], P('seq', 'ch'), may hold values from -6 to 6
- w_in: bfloat16 [8, 1024, 3, 4096], P(None, 'seq', None, 'ch'), may hold values from -0.0625 to 0.0625
- taps: float32 [3, 3, 4096], P(None, None, 'ch'), may hold values from -3.5 to 3.5
- filt: float32 [8192, 4096], P('seq', 'ch'), may hold values from -0.0625 to 0.0625
- bias: float32 [4096], P('ch'), may hold values from -1 to 1
Outputs:
- gated: bfloat16 [8192, 4096], P('seq', 'ch')
All inputs are finite; a program needn't handle non-finite values.
Results may differ from a plain program's by a relative error of at most 0.017.
Values may be sent and summed in bfloat16 or wider, within the bound.
A program may use at most 128 MiB of HBM per device.

v0:
```python
import math

import jax
import jax.numpy as jnp
from jax import lax
from jax.sharding import PartitionSpec as P

HIGH = lax.Precision.HIGHEST


def shifted(value, axis, steps):
    count = lax.axis_size(axis)
    initial, last = (max(0, -steps), min(count, count - steps))
    return lax.ppermute(value, axis, [(source, source + steps) for source in range(initial, last)])


def shortened(x):

    def short(part):
        return part.astype(jnp.bfloat16) if part.dtype == jnp.float32 else part

    return jax.tree.map(short, x)


def table(first, second, modulus):
    angle = (
        2.0 * math.pi * (first[:, None] * second[None, :] % modulus).astype(jnp.float32) / modulus
    )
    return (jnp.cos(angle), jnp.sin(angle))


def on_device(tokens, w_in, taps, filt, bias):
    rows = tokens.shape[0]
    width = filt.shape[1]
    groups = w_in.shape[0]
    whole = lax.all_gather(tokens, "ch", axis=1, tiled=True)
    view = whole.reshape(rows, groups, whole.shape[1] // groups)
    proj = jnp.einsum(
        "tbf,bfjc->tjc",
        view,
        lax.all_gather(w_in, "seq", axis=1, tiled=True),
        preferred_element_type=jnp.float32,
    )
    proj = proj.astype(jnp.bfloat16)
    earlier = shifted(proj[-2:], "seq", 1)
    extended = jnp.concatenate([earlier, proj], axis=0).astype(jnp.float32)
    short = taps[0] * extended[2:] + taps[1] * extended[1:-1] + taps[2] * extended[:-2]
    query = short[:, 0, :]
    signal = short[:, 1, :] * short[:, 2, :]
    parts_count = lax.axis_size("seq")
    myself = lax.axis_index("seq")
    block = rows // parts_count
    freq_rows = 2 * parts_count
    total = 2 * parts_count * rows
    k_small = jnp.arange(freq_rows, dtype=jnp.int32)
    n_small = jnp.arange(parts_count, dtype=jnp.int32)
    positions = jnp.arange(rows, dtype=jnp.int32)
    cos_big, sin_big = table(positions, positions, rows)
    both = jnp.concatenate([signal, filt], axis=1).reshape(1, rows, 2 * width)
    mixed = lax.all_to_all(
        both.astype(jnp.bfloat16), "seq", split_axis=1, concat_axis=0, tiled=True
    ).astype(both.dtype)
    cos_small, sin_small = table(k_small, n_small, freq_rows)
    real_part = jnp.einsum("kn,nmw->mkw", cos_small, mixed, precision=HIGH)
    imag_part = -jnp.einsum("kn,nmw->mkw", sin_small, mixed, precision=HIGH)
    n_global = myself * block + jnp.arange(block, dtype=jnp.int32)
    cos_tw, sin_tw = table(n_global, k_small, total)
    cos_tw = cos_tw[:, :, None]
    sin_tw = sin_tw[:, :, None]
    tw_real = real_part * cos_tw + imag_part * sin_tw
    tw_imag = imag_part * cos_tw - real_part * sin_tw
    spread = lax.all_to_all(
        jnp.stack([tw_real, tw_imag]).astype(jnp.bfloat16),
        "seq",
        split_axis=2,
        concat_axis=1,
        tiled=True,
    ).astype(jnp.float32)
    cos_part = jnp.einsum("kn,rnjw->rkjw", cos_big, spread, precision=HIGH)
    sin_part = jnp.einsum("kn,rnjw->rkjw", sin_big, spread, precision=HIGH)
    spec_real = cos_part[0] + sin_part[1]
    spec_imag = cos_part[1] - sin_part[0]
    sig_real = spec_real[..., :width]
    sig_imag = spec_imag[..., :width]
    fil_real = spec_real[..., width:]
    fil_imag = spec_imag[..., width:]
    prod_real = sig_real * fil_real - sig_imag * fil_imag
    prod_imag = sig_real * fil_imag + sig_imag * fil_real
    product = jnp.stack([prod_real, prod_imag])
    cos_back = jnp.einsum("nk,rkjc->rnjc", cos_big, product, precision=HIGH)
    sin_back = jnp.einsum("nk,rkjc->rnjc", sin_big, product, precision=HIGH)
    z_real = cos_back[0] - sin_back[1]
    z_imag = cos_back[1] + sin_back[0]
    k_mine = 2 * myself + jnp.arange(2, dtype=jnp.int32)
    cos_un, sin_un = table(positions, k_mine, total)
    cos_un = cos_un[:, :, None]
    sin_un = sin_un[:, :, None]
    u_real = z_real * cos_un - z_imag * sin_un
    u_imag = z_imag * cos_un + z_real * sin_un
    back = lax.all_to_all(
        shortened(jnp.stack([u_real, u_imag])), "seq", split_axis=1, concat_axis=2, tiled=True
    )
    cos_last, sin_last = table(n_small, k_small, freq_rows)
    in_time = (
        jnp.einsum("nk,mkc->nmc", cos_last, back[0], precision=HIGH)
        - jnp.einsum("nk,mkc->nmc", sin_last, back[1], precision=HIGH)
    ) / total
    conv = (
        lax.all_to_all(shortened(in_time), "seq", split_axis=0, concat_axis=1, tiled=True)
        .astype(in_time.dtype)
        .reshape(rows, width)
    )
    long_out = conv + bias * signal
    return (query * long_out).astype(jnp.bfloat16)


def solution(mesh):
    return jax.shard_map(
        on_device,
        mesh=mesh,
        in_specs=(
            P("seq", "ch"),
            P(None, "seq", None, "ch"),
            P(None, None, "ch"),
            P("seq", "ch"),
            P("ch"),
        ),
        out_specs=P("seq", "ch"),
        check_vma=False,
    )
```

profile of v0, /device:TPU:2, one launch (start us, length us, event | category | flops | bytes accessed | tf_op | source)
XLA Modules:
  0.0 417.7 jit_solution(3377361204799155644)
XLA Ops:
  6.5 2.1 copy.37
  8.8 1.0 copy.38
  9.8 36.0 %all-gather.3.cloned.1.call-done = bf16[256,8192]{0,1:T(8,128)(2,1)} async-done(((bf16[256,1024]{0,1:T(8,128)(2,1)}), bf16[256,8192]{0,1:T(8,128)(2,1)}) %all-gather.3.cloned.1.call-update) | async-done | bytes 4194320 | tf_op jit(solution)/shard_map/all_gather | solution.py:36
  45.8 187.4 %all-gather.5.cloned.1.call-done = bf16[8,1024,3,512]{3,1,0,2:T(8,128)(2,1)} async-done(((bf16[8,32,3,512]{3,1,0,2:T(8,128)(2,1)}), bf16[8,1024,3,512]{3,1,0,2:T(8,128)(2,1)}) %all-gather.5.cloned.1.call-update) | async-done | bytes 25165840 | tf_op jit(solution)/shard_map/all_gather | solution.py:41
  233.2 12.8 %bitcast_convert_fusion = bf16[256,3,512]{2,0,1:T(8,128)(2,1)S(1)} fusion(bf16[256,8,1024,1]{0,2,1,3:T(8,128)(2,1)} %bitcast.109, bf16[8,1024,3,512]{3,1,0,2:T(8,128)(2,1)} %all-gather.5.cloned.1.call-done), kind=kOutput, calls=%fused_computation.23 | convolution fusion | flops 6442844160 | bytes 30146560 | tf_op jit(solution)/shard_map/tbf,bfjc->tjc/dot_general | solution.py:38
  246.1 2.1 collective-permute-start
  248.2 1.3 collective-permute-done
  250.3 1.1 copy-done
  252.9 3.7 reduce
  256.6 1.1 reshape.186
  257.7 10.3 %all-to-all-start = ((bf16[32,2,4096]{2,1,0:T(2,128)(2,1)}), bf16[32,2,4096]{2,1,0:T(2,128)(2,1)S(1)}, u32[]{:S(2)}, u32[]{:S(2)}) async-start(bf16[32,2,4096]{2,1,0:T(2,128)(2,1)} %reshape.186), calls=%async_computation | async-start | bytes 1048576 | tf_op jit(solution)/shard_map/all_to_all | solution.py:60
  268.2 16.2 %all-to-all-done = bf16[32,2,4096]{2,1,0:T(2,128)(2,1)S(1)} async-done(((bf16[32,2,4096]{2,1,0:T(2,128)(2,1)}), bf16[32,2,4096]{2,1,0:T(2,128)(2,1)S(1)}, u32[]{:S(2)}, u32[]{:S(2)}) %all-to-all-start) | async-done | bytes 524320 | tf_op jit(solution)/shard_map/all_to_all | solution.py:60
  285.1 1.3 fusion.18
  286.4 1.8 fusion.14
  288.4 2.5 copy.43
  290.9 4.4 %all-to-all-start.1 = ((bf16[2,8,64,1024]{3,1,0,2:T(8,128)(2,1)}), bf16[2,8,64,1024]{3,1,0,2:T(8,128)(2,1)S(1)}, u32[]{:S(2)}, u32[]{:S(2)}) async-start(bf16[2,8,64,1024]{3,1,0,2:T(8,128)(2,1)} %copy.43), calls=%async_computation.1 | async-start | bytes 4194304 | tf_op jit(solution)/shard_map/all_to_all | solution.py:72
  295.4 48.3 %all-to-all-done.1 = bf16[2,8,64,1024]{3,1,0,2:T(8,128)(2,1)S(1)} async-done(((bf16[2,8,64,1024]{3,1,0,2:T(8,128)(2,1)}), bf16[2,8,64,1024]{3,1,0,2:T(8,128)(2,1)S(1)}, u32[]{:S(2)}, u32[]{:S(2)}) %all-to-all-start.1) | async-done | bytes 2097184 | tf_op jit(solution)/shard_map/all_to_all | solution.py:72
  343.7 3.4 convolution_bitcast_fusion
  347.1 3.4 convolution_bitcast_fusion.1
  351.5 2.9 fusion.8
  354.3 3.1 fusion.9
  358.0 1.1 copy.48
  359.1 31.4 %all_to_all.54 = bf16[2,256,2,512]{3,2,0,1:T(2,128)(2,1)S(1)} all-to-all(bf16[2,256,2,512]{3,2,0,1:T(2,128)(2,1)S(1)} %copy.48), channel_id=1, replica_groups=mesh['seq'=32,'ch'=8] {'seq'}, dimensions={1} | all-to-all | bytes 2097152 | tf_op jit(solution)/shard_map/all_to_all | solution.py:100
  393.3 16.6 %all_to_all.55 = bf16[32,8,512]{2,1,0:T(8,128)(2,1)S(1)} all-to-all(bf16[32,8,512]{2,1,0:T(8,128)(2,1)S(1)} %copy.52), channel_id=1, replica_groups=mesh['seq'=32,'ch'=8] {'seq'}, dimensions={0} | all-to-all | bytes 524288 | tf_op jit(solution)/shard_map/all_to_all | solution.py:109
  (45 shorter events, 8.5 us)
Async XLA Ops:
  6.5 2.2 copy-start.2
  6.5 3.3 copy-start.3
  6.5 39.3 %all-gather.3.cloned.1.call-start = ((), (), s32[]{:S(2)}) async-start(), calls=%async_computation.4 | async-start | bytes 4718592 | tf_op jit(solution)/shard_map/all_gather | solution.py:36
  8.7 224.5 %all-gather.5.cloned.1.call-start = ((), (), s32[]{:S(2)}) async-start(), calls=%async_computation.5 | async-start | bytes 25952256 | tf_op jit(solution)/shard_map/all_gather | solution.py:41
  233.2 15.0 %copy-start.4 = (f32[3,3,512]{2,1,0:T(4,128)S(1)}, f32[3,3,512]{2,1,0:T(4,128)}, u32[]{:S(2)}) copy-start(f32[3,3,512]{2,1,0:T(4,128)} %param.7) | copy-start | bytes 55300
  246.1 3.5 collective-permute-start
  250.3 1.1 copy-start
  257.7 26.7 %all-to-all-start = ((bf16[32,2,4096]{2,1,0:T(2,128)(2,1)}), bf16[32,2,4096]{2,1,0:T(2,128)(2,1)S(1)}, u32[]{:S(2)}, u32[]{:S(2)}) async-start(bf16[32,2,4096]{2,1,0:T(2,128)(2,1)} %reshape.186), calls=%async_computation | async-start | bytes 1048576 | tf_op jit(solution)/shard_map/all_to_all | solution.py:60
  290.9 52.8 %all-to-all-start.1 = ((bf16[2,8,64,1024]{3,1,0,2:T(8,128)(2,1)}), bf16[2,8,64,1024]{3,1,0,2:T(8,128)(2,1)S(1)}, u32[]{:S(2)}, u32[]{:S(2)}) async-start(bf16[2,8,64,1024]{3,1,0,2:T(8,128)(2,1)} %copy.43), calls=%async_computation.1 | async-start | bytes 4194304 | tf_op jit(solution)/shard_map/all_to_all | solution.py:72
  392.0 18.0 %copy-start.1 = (f32[256,3,512]{2,0,1:T(8,128)S(1)}, f32[256,3,512]{2,0,1:T(8,128)}, u32[]{:S(2)}) copy-start(f32[256,3,512]{2,0,1:T(8,128)} %copy-done) | copy-start | bytes 4718596
  392.0 18.0 %copy-start.5 = (f32[512]{0:T(512)S(1)}, f32[512]{0:T(512)}, u32[]{:S(2)}) copy-start(f32[512]{0:T(512)} %param.9) | copy-start | bytes 6148
Sparse Core Ops, SparseCore 0:
  9.2 36.5 all-gather.2
  48.4 184.7 all-gather.4
where the time goes:
time: 418 us
  waiting for transfers between devices  289 us (69%)
  blocking collectives  48 us (11%)
  matrix products  29.6 us (7%)
  starting transfers between devices  16.8 us (4%)
  between operations  13.7 us (3%)
  local copies, waits for them, and re-layouts  13 us (3%)
  other arithmetic  7.29 us (2%)
    all_gather x1, waiting for transfers between devices, on_device(): lax.all_gather(w_in, 'seq', axis=1, tiled=True)  187 us
    all_to_all x1, waiting for transfers between devices, on_device(): lax.all_to_all(jnp.stack([tw_real, tw_imag]).astype(jnp.bfloat16), 'seq',...  48.3 us
    all_gather x1, waiting for transfers between devices, on_device(): whole = lax.all_gather(tokens, 'ch', axis=1, tiled=True)  36 us
    all_to_all x1, blocking collectives, on_device(): lax.all_to_all(shortened(jnp.stack([u_real, u_imag])), 'seq', split_axis=...  31.4 us
    all_to_all x1, blocking collectives, on_device(): lax.all_to_all(shortened(in_time), 'seq', split_axis=0, concat_axis=1, ti...  16.6 us
    all_to_all x1, waiting for transfers between devices, on_device(): lax.all_to_all(both.astype(jnp.bfloat16), 'seq', split_axis=1, concat_axi...  16.2 us
    dot_general x1, matrix products, on_device(): jnp.einsum('tbf,bfjc->tjc', view, lax.all_gather(w_in, 'seq', axis=1, til...  12.8 us
    all_to_all x1, starting transfers between devices, on_device(): lax.all_to_all(both.astype(jnp.bfloat16), 'seq', split_axis=1, concat_axi...  10.3 us
  transfers between devices with their start and end apart: 5, of which 5 were waited for; matrix products, arithmetic and copies ran while one was open for 0% of the time, Pallas kernels for 0%

commit v1 on v0

v1 whole, which is shorter than its diff:
```python
import functools

import jax
import jax.numpy as jnp
import ml_dtypes
import numpy as np
from jax import lax
from jax.experimental import pallas as pl
from jax.experimental.pallas import tpu as pltpu
from jax.sharding import PartitionSpec as P

MESH = pl.DeviceIdType.MESH
BF = jnp.bfloat16
F32 = jnp.float32

Z, Y, X = 8, 4, 4
ROWS = 256
FEAT = 1024
GROUP = Y * ROWS
CH = 128
CW = CH // Z
WR = 32
N1, N2 = 64, 128
POINTS = N1 * N2
THETA = 0.25
PIECE = (0, -1, 1, 2)


def split(value):
    high = value.astype(ml_dtypes.bfloat16)
    low = (value - high.astype(np.float64)).astype(ml_dtypes.bfloat16)
    return np.stack([high, low])


@functools.cache
def tables():
    k1 = np.arange(N1)[:, None] + THETA
    angle = 2 * np.pi * k1 * np.arange(N1)[None, :] / N1
    first = np.concatenate([np.cos(angle), -np.sin(angle)], axis=0)
    angle = 2 * np.pi * k1 * np.arange(N2)[None, :] / POINTS
    twiddle = np.stack([np.cos(angle), -np.sin(angle)]).astype(np.float32)
    angle = 2 * np.pi * (np.arange(N2)[:, None] * np.arange(N2)[None, :] % N2) / N2
    cos, sin = np.cos(angle), np.sin(angle)
    second = np.block([[cos, -sin], [sin, cos]])
    second_back = np.block([[cos, sin], [-sin, cos]])
    return (
        split(first),
        split(first.T / POINTS),
        twiddle,
        split(second),
        split(second_back),
    )


def dot(a, b):
    return jnp.dot(a, b, preferred_element_type=F32)


def halves(value):
    high = value.astype(BF)
    return high, (value - high.astype(F32)).astype(BF)


def kernel(
    tok_in, w_in, filt, taps, bias, first, first_back, twiddle, second, second_back,
    out,
    tok, wall, acc, proj, halo_out, halo_in, query, signal, sig_t, conv_t, gated,
    filt_t, filt_z, x_in, h_in, spread, stage, high, low, spec_h, y_out,
    send_sem, recv_sem, local_sem,
):
    seq, ch = lax.axis_index("seq"), lax.axis_index("ch")
    z, y, x, core = seq // Y, seq % Y, ch // 2, ch % 2
    numbers = {}

    def number(key):
        return numbers.setdefault(key, len(numbers))

    def device(dz=0, dy=0, dx=0, flip=False):
        to_seq = ((z + dz + Z) % Z) * Y + (y + dy + Y) % Y
        to_ch = ((x + dx + X) % X) * 2 + (1 - core if flip else core)
        return (to_seq, to_ch)

    def remote(key, src, dst, target):
        n = number(key)
        return pltpu.make_async_remote_copy(
            src_ref=src, dst_ref=dst, send_sem=send_sem.at[n], recv_sem=recv_sem.at[n],
            device_id=target, device_id_type=MESH,
        )

    sent = []

    def send(key, src, dst, target):
        copy = remote(key, src, dst, target)
        copy.start()
        sent.append(copy)

    def receive(key, dst):
        remote(key, dst, dst, device(flip=True)).wait_recv()

    def w_place(dz, p):
        return wall.at[(z + dz + Z) % Z, :, pl.ds(((y + PIECE[p] + Y) % Y) * WR, WR), :]

    def t_place(dy, dx, other=False, half=None):
        b = ((x + dx + X) % X) * 2 + (1 - core if other else core)
        start = ((y + dy + Y) % Y) * ROWS
        if half is None:
            return tok.at[b, pl.ds(start, ROWS), :]
        return tok.at[b, pl.ds(start + half * (ROWS // 2), ROWS // 2), :]

    def along(axis, step):
        on_x = (1 - core) if axis == 0 else core
        return step * (1 - on_x), step * on_x

    def shift(axis, step):
        dy, dx = along(axis, step)
        return device(dy=dy, dx=dx)

    own_tok = pltpu.make_async_copy(tok_in, t_place(0, 0), local_sem.at[0])
    own_w = pltpu.make_async_copy(w_in.at[y], w_place(0, 0), local_sem.at[1])
    own_tok.start()
    own_w.start()

    peers = [device(dz=d) for d in range(1, Z)] + [device(dy=d) for d in range(1, Y)]
    peers += [device(dx=1), device(dx=-1), device(flip=True)]
    barrier = pltpu.get_barrier_semaphore()
    for peer in peers:
        pl.semaphore_signal(barrier, inc=1, device_id=peer, device_id_type=MESH)
    pl.semaphore_wait(barrier, len(peers))

    own_w.wait()

    def z_send(d, p, right):
        step = 1 if right else -1
        place = w_place(-step * d, p)
        send(("z", right, d + 1, p), place, place, device(dz=step))

    for p in (1, 2, 3):
        to = -PIECE[p]
        send(
            ("wy", p),
            w_in.at[(y + to + Y) % Y],
            wall.at[z, :, pl.ds(y * WR, WR), :],
            device(dy=to),
        )
        if p == 1:
            z_send(0, 0, True)
            z_send(0, 0, False)

    own_tok.wait()

    OFFSET = (0, 0, 1, -1, 2)

    def block(ring, step, half=None):
        if ring == 0:
            dy, dx = along(0, step)
        else:
            ay, ax = along(0, OFFSET[ring])
            by, bx = along(1, step)
            dy, dx = ay + by, ax + bx
        return t_place(dy + Y, dx + X, half=half)

    def t_send(ring, right, half, d):
        step = 1 if right else -1
        place = block(ring, -step * d, half)
        send(("t", ring, right, half, d + 1), place, place, shift(0 if ring == 0 else 1, step))

    def to_sibling(ring, step):
        place = block(ring, step)
        send(("s", ring, step), place, place, device(flip=True))

    def begin(ring):
        t_send(ring, True, 0, 0)
        t_send(ring, False, 1, 0)
        t_send(ring, True, 1, 0)
        t_send(ring, False, 0, 0)

    def near_first(ring):
        receive(("t", ring, True, 0, 1), block(ring, -1, 0))
        t_send(ring, True, 0, 1)
        receive(("t", ring, False, 1, 1), block(ring, 1, 1))
        t_send(ring, False, 1, 1)

    def near_second(ring):
        receive(("t", ring, True, 1, 1), block(ring, -1, 1))
        receive(("t", ring, False, 0, 1), block(ring, 1, 0))
        to_sibling(ring, -1)
        to_sibling(ring, 1)

    def far(ring):
        receive(("t", ring, True, 0, 2), block(ring, 2, 0))
        receive(("t", ring, False, 1, 2), block(ring, 2, 1))
        to_sibling(ring, 2)

    begin(0)
    begin(1)
    to_sibling(0, 0)

    for i in range(2):
        for quarter in range(4):
            part = filt[i * N2:(i + 1) * N2, quarter * CH:(quarter + 1) * CH]
            filt_t[i, quarter * CH:(quarter + 1) * CH, :] = part.T.astype(BF)
    for d in range(1, Y):
        to = (y + d) % Y
        send(
            ("fy", d),
            filt_t.at[:, pl.ds(to * CH, CH), :],
            filt_z.at[pl.ds(2 * y, 2), :, :],
            device(dy=d),
        )
    filt_z[pl.ds(2 * y, 2), :, :] = filt_t[:, pl.ds(pl.multiple_of(y * CH, CH), CH), :]
    acc[...] = jnp.zeros_like(acc)

    for p in (1, 2, 3):
        receive(("wy", p), w_place(0, p))
        z_send(0, p, True)
        z_send(0, p, False)

    def across(name, src, dst):
        for d in range(1, Z):
            to = (z + d) % Z
            send(
                (name, d),
                src.at[:, pl.ds(to * CW, CW), :],
                dst.at[pl.ds(z * Z, Z), :, :],
                device(dz=d),
            )
        dst[pl.ds(z * Z, Z), :, :] = src[:, pl.ds(pl.multiple_of(z * CW, CW), CW), :]

    def across_wait(name, dst):
        for d in range(1, Z):
            receive((name, d), dst.at[pl.ds(((z - d + Z) % Z) * Z, Z), :, :])

    def transform(source):
        spread[...] = source[...].astype(F32).reshape(N1 * CW, N2)
        for c in range(0, CW, 2):
            both = jnp.concatenate(
                [spread[pl.ds(c + s, N1, stride=CW), :].astype(BF) for s in range(2)], axis=1
            )
            part = dot(first[0], both) + dot(first[1], both)
            for s in range(2):
                re, im = part[:N1, s * N2:(s + 1) * N2], part[N1:, s * N2:(s + 1) * N2]
                turned = jnp.concatenate(
                    [re * twiddle[0] - im * twiddle[1], re * twiddle[1] + im * twiddle[0]], axis=1
                )
                rows = pl.ds((c + s) * N1, N1)
                high[rows, :], low[rows, :] = halves(turned)
        product(second)

    def product(matrix):
        def rows_of(i, carry):
            rows = pl.ds(pl.multiple_of(i * 256, 256), 256)
            stage[rows, :] = dot(high[rows, :], matrix[0]) + (
                dot(low[rows, :], matrix[0]) + dot(high[rows, :], matrix[1])
            )
            return carry

        lax.fori_loop(0, CW * N1 // 256, rows_of, 0)

    def filter_across():
        for d in range(1, Y):
            receive(("fy", d), filt_z.at[pl.ds(2 * ((y - d + Y) % Y), 2), :, :])
        across("fz", filt_z, h_in)

    def filter_transform():
        across_wait("fz", h_in)
        transform(h_in)
        spec_h[...] = stage[...]

    def next_rings():
        begin(2)
        begin(3)

    def last_ring():
        begin(4)

    between = {
        0: [lambda: near_first(0), lambda: near_second(0), next_rings],
        1: [lambda: far(0), last_ring, lambda: near_first(1)],
        2: [lambda: near_second(1), lambda: far(1)],
        3: [lambda: near_first(2), lambda: near_second(2), filter_across],
        4: [lambda: far(2)],
        5: [lambda: near_first(3), lambda: near_second(3)],
        6: [lambda: far(3), filter_transform],
        7: [lambda: near_first(4)],
        8: [lambda: near_second(4)],
        9: [lambda: far(4)],
    }
    for d in range(1, 4):
        for p in range(4):
            for event in between.get((d - 1) * 4 + p, []):
                event()
            receive(("z", True, d, p), w_place(-d, p))
            if d < 3 or p < 2:
                z_send(d, p, True)
            receive(("z", False, d, p), w_place(d, p))
            if d < 3 or p >= 2:
                z_send(d, p, False)

    for ring in range(5):
        for step in ((0, -1, 1, 2) if ring == 0 else (-1, 1, 2)):
            if ring == 0:
                dy, dx = step * (1 - core), step * core
            else:
                dy = OFFSET[ring] * (1 - core) + step * core
                dx = OFFSET[ring] * core + step * (1 - core)
            receive(("s", ring, step), t_place(dy + Y, dx + X, other=True))

    def chunk(source, rows):
        left = jnp.concatenate(
            [
                tok[b, rows, pl.ds(pl.multiple_of(source * N2, N2), N2)]
                for b in range(2 * X)
            ],
            axis=1,
        )
        return dot(left, wall[source].reshape(FEAT, 3 * CH))

    def gather_sum(n, carry):
        source = (z + 5 + n // 4) % Z
        rows = pl.ds(pl.multiple_of((n % 4) * ROWS, ROWS), ROWS)
        acc[rows, :] += chunk(source, rows)
        return carry

    lax.fori_loop(0, 28, gather_sum, 0)
    for p in range(4):
        receive(("z", p < 2, 4, p), w_place(4, p))

    for part in (3, 0, 1, 2):
        rows = pl.ds(part * ROWS, ROWS)
        rounded = (acc[rows, :] + chunk((z + 4) % Z, rows)).astype(BF)
        proj[pl.ds(8 + part * ROWS, ROWS), :] = rounded.astype(F32)
        if part == 3:
            halo_out[...] = rounded[ROWS - 16:, :]
            send(("halo",), halo_out, halo_in, device(dz=1))

    mine = pl.ds(pl.multiple_of(y * CH, CH), CH)

    def short(i, j):
        columns = slice(j * CH, (j + 1) * CH)
        return sum(
            taps[s, j:j + 1, mine] * proj[pl.ds(8 - s + i * N2, N2), columns] for s in range(3)
        )

    for i in reversed(range(8)):
        if i == 0:
            receive(("halo",), halo_in)
            before = halo_in[...].astype(F32)[8:, :]
            proj[:8, :] = jnp.where(z > 0, before, 0.0)
        rows = pl.ds(i * N2, N2)
        query[rows, :] = short(i, 0)
        value = short(i, 1) * short(i, 2)
        signal[rows, :] = value
        sig_t[i] = value.T.astype(BF)

    across("sz", sig_t, x_in)
    across_wait("sz", x_in)
    transform(x_in)

    def multiply(i, carry):
        rows = pl.ds(pl.multiple_of(i * N1, N1), N1)
        a_re, a_im = stage[rows, :N2], stage[rows, N2:]
        b_re, b_im = spec_h[rows, :N2], spec_h[rows, N2:]
        high[rows, :], low[rows, :] = halves(
            jnp.concatenate([a_re * b_re - a_im * b_im, a_re * b_im + a_im * b_re], axis=1)
        )
        return carry

    lax.fori_loop(0, CW, multiply, 0)
    product(second_back)
    for c in range(0, CW, 2):
        turned = []
        for s in range(2):
            rows = pl.ds((c + s) * N1, N1)
            re, im = stage[rows, :N2], stage[rows, N2:]
            turned.append(
                jnp.concatenate(
                    [re * twiddle[0] + im * twiddle[1], im * twiddle[0] - re * twiddle[1]], axis=0
                )
            )
        top, rest = halves(jnp.concatenate(turned, axis=1))
        part = dot(first_back[0], top) + (dot(first_back[0], rest) + dot(first_back[1], top))
        for s in range(2):
            spread[pl.ds(c + s, N1, stride=CW), :] = part[:, s * N2:(s + 1) * N2]
    y_out[...] = spread[...].astype(BF).reshape(N1, CW, N2)

    for d in range(1, Z):
        to = (z + d) % Z
        send(
            ("yz", d),
            y_out.at[pl.ds(to * Z, Z), :, :],
            conv_t.at[:, pl.ds(z * CW, CW), :],
            device(dz=d),
        )
    conv_t[:, pl.ds(pl.multiple_of(z * CW, CW), CW), :] = y_out[pl.ds(z * Z, Z), :, :]
    for d in range(1, Z):
        receive(("yz", d), conv_t.at[:, pl.ds(((z - d + Z) % Z) * CW, CW), :])

    for d in (2, 1, 3, 0):
        to = (y + d) % Y
        for i in range(2):
            rows = pl.ds(pl.multiple_of(to * ROWS + i * N2, N2), N2)
            conv = conv_t[2 * to + i].astype(F32).T
            gated[rows, :] = (
                query[rows, :] * (conv + bias[:, mine] * signal[rows, :])
            ).astype(BF)
        rows = pl.ds(pl.multiple_of(to * ROWS, ROWS), ROWS)
        if d:
            send(("out", d), gated.at[rows, :], out.at[:, mine], device(dy=d))
        else:
            out[:, mine] = gated[rows, :]
    for d in range(1, Y):
        columns = pl.ds(pl.multiple_of(((y - d + Y) % Y) * CH, CH), CH)
        receive(("out", d), out.at[:, columns])
    for copy in sent:
        copy.wait_send()


COPIES = 3 + 28 + 30 + 16 + 3 + 7 + 7 + 1 + 7 + 3


def on_device(tokens, w_in, taps, filt, bias):
    w_parts = w_in.reshape(2 * X, WR, 3, Y, CH).transpose(3, 0, 1, 2, 4)
    w_parts = w_parts.reshape(Y, 2 * X, WR, 3 * CH)
    any_space = pl.BlockSpec(memory_space=pl.ANY)
    vmem = pl.BlockSpec(memory_space=pltpu.VMEM)
    scratch = [
        pltpu.VMEM((2 * X, GROUP, FEAT), BF),
        pltpu.VMEM((Z, 2 * X, Y * WR, 3 * CH), BF),
        pltpu.VMEM((GROUP, 3 * CH), F32),
        pltpu.VMEM((GROUP + 8, 3 * CH), F32),
        pltpu.VMEM((16, 3 * CH), BF),
        pltpu.VMEM((16, 3 * CH), BF),
        pltpu.VMEM((GROUP, CH), F32),
        pltpu.VMEM((GROUP, CH), F32),
        pltpu.VMEM((8, CH, N2), BF),
        pltpu.VMEM((8, CH, N2), BF),
        pltpu.VMEM((GROUP, CH), BF),
        pltpu.VMEM((2, Y * CH, N2), BF),
        pltpu.VMEM((8, CH, N2), BF),
        pltpu.VMEM((N1, CW, N2), BF),
        pltpu.VMEM((N1, CW, N2), BF),
        pltpu.VMEM((N1 * CW, N2), F32),
        pltpu.VMEM((CW * N1, 2 * N2), F32),
        pltpu.VMEM((CW * N1, 2 * N2), BF),
        pltpu.VMEM((CW * N1, 2 * N2), BF),
        pltpu.VMEM((CW * N1, 2 * N2), F32),
        pltpu.VMEM((N1, CW, N2), BF),
        pltpu.SemaphoreType.DMA((COPIES,)),
        pltpu.SemaphoreType.DMA((COPIES,)),
        pltpu.SemaphoreType.DMA((2,)),
    ]
    return pl.pallas_call(
        kernel,
        out_shape=jax.ShapeDtypeStruct((ROWS, Y * CH), BF),
        in_specs=[any_space, any_space] + [vmem] * 8,
        out_specs=vmem,
        scratch_shapes=scratch,
        compiler_params=pltpu.CompilerParams(
            collective_id=0, has_side_effects=True, vmem_limit_bytes=50 * 1024 * 1024
        ),
        name="layer",
    )(tokens, w_parts, filt, taps, bias[None, :], *(jnp.asarray(t) for t in tables()))


def solution(mesh):
    return jax.shard_map(
        on_device,
        mesh=mesh,
        in_specs=(
            P("seq", "ch"),
            P(None, "seq", None, "ch"),
            P(None, None, "ch"),
            P("seq", "ch"),
            P("ch"),
        ),
        out_specs=P("seq", "ch"),
        check_vma=False,
    )
```

time: 418 us -> 138 us (0.33)
  waiting for transfers between devices: 289 us -> 0 us
  Pallas kernels: 0 us -> 131 us
  blocking collectives: 48 us -> 0 us
  matrix products: 29.6 us -> 0 us
  starting transfers between devices: 16.8 us -> 0 us
  between operations: 13.7 us -> 0.14 us
  other arithmetic: 7.29 us -> 0 us
  local copies, waits for them, and re-layouts: 13 us -> 6.71 us
    all_gather x2 -> x0, waiting for transfers between devices: 223 us -> none  [the longest x1 187 us: on_device(): lax.all_gather(w_in, 'seq', axis=1, tiled=True)]
    pallas_call x0 -> x1, Pallas kernels: none -> 131 us  [on_device(): pl.pallas_call(kernel, out_shape=jax.ShapeDtypeStruct((ROWS, Y * CH), BF)...]
    all_to_all x2 -> x0, waiting for transfers between devices: 64.5 us -> none  [the longest x1 48.3 us: on_device(): lax.all_to_all(jnp.stack([tw_real, tw_imag]).astype(jnp.bfloat16), 'seq',...]
    all_to_all x2 -> x0, blocking collectives: 48 us -> none  [the longest x1 31.4 us: on_device(): lax.all_to_all(shortened(jnp.stack([u_real, u_imag])), 'seq', split_axis=...]
    dot_general x9 -> x0, matrix products: 29.6 us -> none  [the longest x1 12.8 us: on_device(): jnp.einsum('tbf,bfjc->tjc', view, lax.all_gather(w_in, 'seq', axis=1, til...]
    all_to_all x2 -> x0, starting transfers between devices: 14.7 us -> none  [the longest x1 10.3 us: on_device(): lax.all_to_all(both.astype(jnp.bfloat16), 'seq', split_axis=1, concat_axi...]
    reshape x0 -> x3, local copies, waits for them, and re-layouts: none -> 5.95 us  [the longest x2 3.39 us: on_device(): w_parts = w_in.reshape(2 * X, WR, 3, Y, CH).transpose(3, 0, 1, 2, 4)]
    unnamed x18 -> x19, local copies, waits for them, and re-layouts: 6.66 us -> 0.75 us
  transfers between devices with their start and end apart: 5 -> 0, of which waited for: 5 -> 0; matrix products, arithmetic and copies ran while one was open for 0% -> 0% of each run, Pallas kernels for 0% -> 0%
where the time goes in v1:
time: 138 us
  Pallas kernels  131 us (95%)
  local copies, waits for them, and re-layouts  6.71 us (5%)
    pallas_call x1, Pallas kernels, on_device(): pl.pallas_call(kernel, out_shape=jax.ShapeDtypeStruct((ROWS, Y * CH), BF)...  131 us
    reshape x2, local copies, waits for them, and re-layouts, on_device(): w_parts = w_in.reshape(2 * X, WR, 3, Y, CH).transpose(3, 0, 1, 2, 4)  3.39 us

profile of v1, /device:TPU:2, one launch (start us, length us, event | category | flops | bytes accessed | tf_op | source)
XLA Modules:
  0.0 137.8 jit_solution(9804917294760009673)
XLA Ops:
  0.0 1.7 %reshape.6 = bf16[8,32,3,4,128]{4,3,1,2,0:T(4,128)(2,1)S(1)} reshape(bf16[8,32,3,512]{3,1,2,0:T(8,128)(2,1)} %param.11) | data formatting | bytes 1572864 | tf_op jit(solution)/shard_map/reshape | solution.py:422
  1.8 1.6 %copy.14 = bf16[8,32,3,4,128]{4,2,1,0,3:T(4,128)(2,1)} copy(bf16[8,32,3,4,128]{4,3,1,2,0:T(4,128)(2,1)S(1)} %reshape.6) | data formatting | bytes 1572864 | tf_op jit(solution)/shard_map/reshape | solution.py:422
  3.4 0.0 copy-start
  3.4 0.0 copy-start.1
  3.4 0.0 copy-start.2
  3.4 0.0 copy-start.3
  3.4 0.0 copy-start.4
  3.4 0.0 copy-start.5
  3.4 0.0 copy-start.6
  3.4 0.0 copy-start.7
  3.5 0.0 copy-start.8
  3.5 2.6 %reshape.7.w_in = bf16[4,8,32,384]{3,2,1,0:T(8,128)(2,1)S(1)} reshape(bf16[4,8,32,3,128]{4,3,2,1,0:T(4,128)(2,1)} %bitcast.9) | data formatting | bytes 1572864 | tf_op jit(solution)/shard_map/reshape | solution.py:423
  6.0 0.0 copy-done
  6.1 0.0 copy-done.1
  6.1 0.0 copy-done.2
  6.1 0.0 copy-done.3
  6.1 0.0 copy-done.4
  6.1 0.0 copy-done.5
  6.1 0.0 copy-done.6
  6.1 0.0 copy-done.7
  6.1 0.0 copy-done.8
  6.1 131.0 %layer.1 = bf16[256,512]{1,0:T(8,128)(2,1)S(1)} custom-call(bf16[256,1024]{1,0:T(8,128)(2,1)S(1)} %copy-done, bf16[4,8,32,384]{3,2,1,0:T(8,128)(2,1)S(1)} %reshape.7.w_in, f32[256,512]{1,0:T(8,128)S(1)} %copy-done.1, f32[3,3,512]{2,1,0:T(4,128)S(1)} %copy-done.7, f32[1,512]{1,0:T(1,128)S(1)} %bitcast.8, bf16[2,128,64]{2,1,0:T(8,128)(2,1)S(1)} %copy-done.5, ...), custom_call_target="tpu_custom_call" | custom-call | tf_op jit(solution)/shard_map/layer/pallas_call | solution.py:452
  137.1 0.7 copy.16
Async XLA Ops:
  3.4 2.6 %copy-start = (bf16[256,1024]{1,0:T(8,128)(2,1)S(1)}, bf16[256,1024]{1,0:T(8,128)(2,1)}, u32[]{:S(2)}) copy-start(bf16[256,1024]{1,0:T(8,128)(2,1)} %tok_in.1) | copy-start | bytes 1572868
  3.4 2.7 %copy-start.1 = (f32[256,512]{1,0:T(8,128)S(1)}, f32[256,512]{1,0:T(8,128)}, u32[]{:S(2)}) copy-start(f32[256,512]{1,0:T(8,128)} %filt.1) | copy-start | bytes 1572868
  3.4 2.7 %copy-start.2 = (bf16[2,256,256]{2,1,0:T(8,128)(2,1)S(1)}, bf16[2,256,256]{2,1,0:T(8,128)(2,1)}, u32[]{:S(2)}) copy-start(bf16[2,256,256]{2,1,0:T(8,128)(2,1)} %constant.14.clone.second_back) | copy-start | bytes 786436
  3.4 2.7 %copy-start.3 = (bf16[2,256,256]{2,1,0:T(8,128)(2,1)S(1)}, bf16[2,256,256]{2,1,0:T(8,128)(2,1)}, u32[]{:S(2)}) copy-start(bf16[2,256,256]{2,1,0:T(8,128)(2,1)} %constant.13.clone.second) | copy-start | bytes 786436
  3.4 2.7 %copy-start.4 = (f32[2,64,128]{2,1,0:T(8,128)S(1)}, f32[2,64,128]{2,1,0:T(8,128)}, u32[]{:S(2)}) copy-start(f32[2,64,128]{2,1,0:T(8,128)} %constant.12.clone.twiddle) | copy-start | bytes 196612
  3.4 2.7 %copy-start.5 = (bf16[2,128,64]{2,1,0:T(8,128)(2,1)S(1)}, bf16[2,128,64]{2,1,0:T(8,128)(2,1)}, u32[]{:S(2)}) copy-start(bf16[2,128,64]{2,1,0:T(8,128)(2,1)} %constant.10.clone.first) | copy-start | bytes 98308
  3.4 2.7 %copy-start.6 = (bf16[2,64,128]{2,1,0:T(8,128)(2,1)S(1)}, bf16[2,64,128]{2,1,0:T(8,128)(2,1)}, u32[]{:S(2)}) copy-start(bf16[2,64,128]{2,1,0:T(8,128)(2,1)} %constant.11.clone.first_back) | copy-start | bytes 98308
  3.4 2.7 %copy-start.7 = (f32[3,3,512]{2,1,0:T(4,128)S(1)}, f32[3,3,512]{2,1,0:T(4,128)}, u32[]{:S(2)}) copy-start(f32[3,3,512]{2,1,0:T(4,128)} %taps.1) | copy-start | bytes 55300
  3.5 2.7 %copy-start.8 = (f32[512]{0:T(512)S(1)}, f32[512]{0:T(512)}, u32[]{:S(2)}) copy-start(f32[512]{0:T(512)} %param.14) | copy-start | bytes 6148

commit v2 on v1

v2 whole, which is shorter than its diff:
```python
import functools

import jax
import jax.numpy as jnp
import ml_dtypes
import numpy as np
from jax import lax
from jax.experimental import pallas as pl
from jax.experimental.pallas import tpu as pltpu
from jax.sharding import PartitionSpec as P

MESH = pl.DeviceIdType.MESH
BF = jnp.bfloat16
F32 = jnp.float32

Z, Y, X = 8, 4, 4
ROWS = 256
FEAT = 1024
GROUP = Y * ROWS
CH = 128
PARTS = 2
CW = CH // Z // PARTS
WR = 32
N1, N2 = 64, 128
POINTS = N1 * N2
THETA = 0.25
FAR_FIRST = (4, 3, 5, 2, 6, 1, 7)
PIECE = (0, -1, 1, 2)


def split(value):
    high = value.astype(ml_dtypes.bfloat16)
    low = (value - high.astype(np.float64)).astype(ml_dtypes.bfloat16)
    return np.stack([high, low])


@functools.cache
def tables():
    k1 = np.arange(N1)[:, None] + THETA
    angle = 2 * np.pi * k1 * np.arange(N1)[None, :] / N1
    first = np.concatenate([np.cos(angle), -np.sin(angle)], axis=0)
    angle = 2 * np.pi * k1 * np.arange(N2)[None, :] / POINTS
    twiddle = np.stack([np.cos(angle), -np.sin(angle)]).astype(np.float32)
    angle = 2 * np.pi * (np.arange(N2)[:, None] * np.arange(N2)[None, :] % N2) / N2
    cos, sin = np.cos(angle), np.sin(angle)
    second = split(np.block([[cos, -sin], [sin, cos]]))
    second_back = split(np.block([[cos, sin], [-sin, cos]]))
    first_back = split(first.T / POINTS)
    return (
        np.concatenate(list(split(first)), axis=1),
        np.concatenate([first_back[0], first_back[0], first_back[1]], axis=1),
        twiddle,
        np.concatenate([second[0], second[0], second[1]], axis=0),
        np.concatenate([second_back[0], second_back[0], second_back[1]], axis=0),
    )


def dot(a, b):
    return jnp.dot(a, b, preferred_element_type=F32)


def halves(value):
    high = value.astype(BF)
    return high, (value - high.astype(F32)).astype(BF)


def by_channel(even, odd):
    turned = [value.T.reshape(CH // CW, CW, N2) for value in (even, odd)]
    return jnp.concatenate(turned, axis=1).astype(BF).reshape(PARTS, Z, 2 * CW, N2)


def kernel(
    tok_in, w_in, filt_in, taps_in, bias_in, first_in, first_back_in, twiddle_in, second_in,
    second_back_in, out,
    filt, taps, bias, first, first_back, twiddle, second, second_back, tok, wall, acc, proj, halo_out, halo_in, query, signal, sig_t, conv_t, gated,
    filt_t, filt_z, x_in, h_in, spread, stage, split_rows, spec_h, y_out,
    send_sem, recv_sem, local_sem,
):
    seq, ch = lax.axis_index("seq"), lax.axis_index("ch")
    z, y, x, core = seq // Y, seq % Y, ch // 2, ch % 2
    numbers = {}

    def number(key):
        return numbers.setdefault(key, len(numbers))

    def device(dz=0, dy=0, dx=0, flip=False):
        to_seq = ((z + dz + Z) % Z) * Y + (y + dy + Y) % Y
        to_ch = ((x + dx + X) % X) * 2 + (1 - core if flip else core)
        return (to_seq, to_ch)

    def remote(key, src, dst, target):
        n = number(key)
        return pltpu.make_async_remote_copy(
            src_ref=src, dst_ref=dst, send_sem=send_sem.at[n], recv_sem=recv_sem.at[n],
            device_id=target, device_id_type=MESH,
        )

    sent = []

    def send(key, src, dst, target):
        copy = remote(key, src, dst, target)
        copy.start()
        sent.append(copy)

    def receive(key, dst):
        remote(key, dst, dst, device(flip=True)).wait_recv()

    def w_place(dz, p):
        return wall.at[(z + dz + Z) % Z, :, pl.ds(((y + PIECE[p] + Y) % Y) * WR, WR), :]

    def t_place(dy, dx, other=False, half=None):
        b = ((x + dx + X) % X) * 2 + (1 - core if other else core)
        start = ((y + dy + Y) % Y) * ROWS
        if half is None:
            return tok.at[b, pl.ds(start, ROWS), :]
        return tok.at[b, pl.ds(start + half * (ROWS // 2), ROWS // 2), :]

    def along(axis, step):
        on_x = (1 - core) if axis == 0 else core
        return step * (1 - on_x), step * on_x

    def shift(axis, step):
        dy, dx = along(axis, step)
        return device(dy=dy, dx=dx)

    own_tok = pltpu.make_async_copy(tok_in, t_place(0, 0), local_sem.at[0])
    def w_columns(to, j):
        return w_in.at[j, :, :, pl.ds(to * CH, CH)]

    def w_home(j):
        return wall.at[z, :, pl.ds(y * WR, WR), pl.ds(j * CH, CH)]

    own_w = [pltpu.make_async_copy(w_columns(y, j), w_home(j), local_sem.at[1 + j]) for j in range(3)]
    pairs = [(filt_in, filt), (taps_in, taps), (bias_in, bias), (first_in, first), (first_back_in, first_back)]
    pairs += [(twiddle_in, twiddle), (second_in, second), (second_back_in, second_back)]
    own = [pltpu.make_async_copy(a, b, local_sem.at[4 + n]) for n, (a, b) in enumerate(pairs)]
    for copy in own[:1] + own_w + [own_tok] + own[1:]:
        copy.start()

    peers = [device(dz=d) for d in range(1, Z)] + [device(dy=d) for d in range(1, Y)]
    peers += [device(dx=1), device(dx=-1), device(flip=True)]
    barrier = pltpu.get_barrier_semaphore()
    for peer in peers:
        pl.semaphore_signal(barrier, inc=1, device_id=peer, device_id_type=MESH)

    own[0].wait()
    for quarter in range(Y):
        columns = slice(quarter * CH, (quarter + 1) * CH)
        filt_t[quarter] = by_channel(filt[:N2, columns], filt[N2:, columns])
    acc[...] = jnp.zeros_like(acc)

    pl.semaphore_wait(barrier, len(peers))

    for copy in own_w:
        copy.wait()

    def z_send(d, p, right):
        step = 1 if right else -1
        place = w_place(-step * d, p)
        send(("z", right, d + 1, p), place, place, device(dz=step))

    def w_send(p):
        to = -PIECE[p]
        for j in range(3):
            send(("wy", p, j), w_columns((y + to + Y) % Y, j), w_home(j), device(dy=to))

    z_send(0, 0, True)
    z_send(0, 0, False)
    w_send(1)
    w_send(2)
    own_tok.wait()
    for copy in own[1:]:
        copy.wait()

    OFFSET = (0, 0, 1, -1, 2)

    def block(ring, step, half=None):
        if ring == 0:
            dy, dx = along(0, step)
        else:
            ay, ax = along(0, OFFSET[ring])
            by, bx = along(1, step)
            dy, dx = ay + by, ax + bx
        return t_place(dy + Y, dx + X, half=half)

    def t_send(ring, right, half, d):
        step = 1 if right else -1
        place = block(ring, -step * d, half)
        send(("t", ring, right, half, d + 1), place, place, shift(0 if ring == 0 else 1, step))

    def to_sibling(ring, step):
        place = block(ring, step)
        send(("s", ring, step), place, place, device(flip=True))

    def begin(ring):
        t_send(ring, True, 0, 0)
        t_send(ring, False, 1, 0)
        t_send(ring, True, 1, 0)
        t_send(ring, False, 0, 0)

    def begin_a(ring):
        t_send(ring, True, 0, 0)
        t_send(ring, False, 1, 0)

    def begin_b(ring):
        t_send(ring, True, 1, 0)
        t_send(ring, False, 0, 0)

    def near_first(ring):
        receive(("t", ring, True, 0, 1), block(ring, -1, 0))
        t_send(ring, True, 0, 1)
        receive(("t", ring, False, 1, 1), block(ring, 1, 1))
        t_send(ring, False, 1, 1)

    def near_second(ring):
        receive(("t", ring, True, 1, 1), block(ring, -1, 1))
        receive(("t", ring, False, 0, 1), block(ring, 1, 0))
        to_sibling(ring, -1)
        to_sibling(ring, 1)

    def far(ring):
        receive(("t", ring, True, 0, 2), block(ring, 2, 0))
        receive(("t", ring, False, 1, 2), block(ring, 2, 1))
        to_sibling(ring, 2)

    begin_a(0)
    w_send(3)
    begin_b(0)
    to_sibling(0, 0)

    def across(name, part, src, dst):
        for d in FAR_FIRST:
            send(
                (name, part, d),
                src.at[:, part, (z + d) % Z],
                dst.at[part, pl.ds(z * Y, Y)],
                device(dz=d),
            )
        dst[part, pl.ds(z * Y, Y)] = src[:, part, z]

    def across_wait(name, part, dst):
        for d in range(1, Z):
            receive((name, part, d), dst.at[part, pl.ds(((z - d + Z) % Z) * Y, Y)])

    def transform(source, part):
        spread[...] = source[part].astype(F32).reshape(N1 * CW, N2)
        together = jnp.concatenate(
            [spread[pl.ds(c, N1, stride=CW), :].astype(BF) for c in range(CW)], axis=1
        )
        values = dot(first[...], jnp.concatenate([together, together], axis=0))
        for c in range(CW):
            columns = slice(c * N2, (c + 1) * N2)
            re, im = values[:N1, columns], values[N1:, columns]
            turned = jnp.concatenate(
                [re * twiddle[0] - im * twiddle[1], re * twiddle[1] + im * twiddle[0]], axis=1
            )
            in_halves(c, turned)
        stage[...] = dot(split_rows[...], second[...])

    def in_halves(c, value):
        rows = pl.ds(c * N1, N1)
        top, rest = halves(value)
        split_rows[rows, :2 * N2] = top
        split_rows[rows, 2 * N2:4 * N2] = rest
        split_rows[rows, 4 * N2:] = top

    def filter_across():
        for d in range(1, Y):
            receive(("fy", d), filt_z.at[(y - d + Y) % Y])
        for part in range(PARTS):
            across("fz", part, filt_z, h_in)

    def filter_transform(part):
        across_wait("fz", part, h_in)
        transform(h_in, part)
        spec_h[part] = stage[...]

    def filter_send():
        for d in range(1, Y):
            send(("fy", d), filt_t.at[(y + d) % Y], filt_z.at[y], device(dy=d))
        filt_z[y] = filt_t[y]

    def w_next(p):
        for j in range(3):
            columns = pl.ds(j * CH, CH)
            rows = pl.ds(((y + PIECE[p] + Y) % Y) * WR, WR)
            receive(("wy", p, j), wall.at[z, :, rows, columns])
        z_send(0, p, True)
        z_send(0, p, False)

    def z_next(s):
        d, p = s // 4 + 1, s % 4
        receive(("z", True, d, p), w_place(-d, p))
        if d < 3 or p < 2:
            z_send(d, p, True)
        receive(("z", False, d, p), w_place(d, p))
        if d < 3 or p >= 2:
            z_send(d, p, False)

    def total(blocks, rows, offsets):
        left, right = [], []
        for offset in offsets:
            source = (z + offset + Z) % Z
            for b in blocks:
                left.append(tok[b, rows, pl.ds(pl.multiple_of(source * N2, N2), N2)])
                right.append(wall[source, b])
        return acc[rows, :] + dot(jnp.concatenate(left, axis=1), jnp.concatenate(right, axis=0))

    EARLY = (0, -1, 1, -2, 2)
    LATE = (-3, 3)

    def unit(ring):
        for step in (-1, 1, 2):
            dy = OFFSET[ring] * (1 - core) + step * core
            dx = OFFSET[ring] * core + step * (1 - core)
            receive(("s", ring, step), t_place(dy + Y, dx + X, other=True))
        step = OFFSET[ring]
        receive(("s", 0, step), t_place(step * (1 - core) + Y, step * core + X, other=True))
        column = (x + OFFSET[ring] + X) % X

        def rows_of(n, carry):
            rows = pl.ds(pl.multiple_of(n * ROWS, ROWS), ROWS)
            acc[rows, :] = total([column * 2], rows, EARLY)
            return carry

        lax.fori_loop(0, Y, rows_of, 0)
        rows = pl.ds(pl.multiple_of(((y + OFFSET[ring] + Y) % Y) * ROWS, ROWS), ROWS)
        acc[rows, :] = total([2 * b + 1 for b in range(X)], rows, EARLY)

    def late():
        def rows_of(n, carry):
            rows = pl.ds(pl.multiple_of(n * ROWS, ROWS), ROWS)
            acc[rows, :] = total(range(2 * X), rows, LATE)
            return carry

        lax.fori_loop(0, Y, rows_of, 0)

    order = [
        (w_next, 1), (w_next, 2), (near_first, 0), (begin, 1), (filter_send,), (w_next, 3), (z_next, 0),
        (near_second, 0), (begin, 2), (begin, 3), (near_first, 1), (z_next, 1), (near_second, 1), (z_next, 2),
        (z_next, 3), (near_first, 2), (far, 0), (begin, 4), (near_second, 2), (z_next, 4),
        (near_first, 3), (z_next, 5), (near_second, 3), (near_first, 4), (z_next, 6),
        (near_second, 4), (z_next, 7), (far, 1), (far, 2), (z_next, 8), (far, 3), (z_next, 9),
        (far, 4), (z_next, 10), (z_next, 11), (filter_across,), (unit, 1), (unit, 2), (unit, 3), (unit, 4),
        (late,),
    ]
    for event, *values in order:
        event(*values)

    for p in range(4):
        receive(("z", p < 2, 4, p), w_place(4, p))

    for n in (3, 0, 1, 2):
        rounded = total(range(2 * X), pl.ds(n * ROWS, ROWS), (4,)).astype(BF)
        proj[pl.ds(8 + n * ROWS, ROWS), :] = rounded.astype(F32)
        if n == 3:
            halo_out[...] = rounded[ROWS - 16:, :]
            send(("halo",), halo_out, halo_in, device(dz=1))

    mine = pl.ds(pl.multiple_of(y * CH, CH), CH)

    def short(start, j):
        columns = slice(j * CH, (j + 1) * CH)
        return sum(
            taps[s, j:j + 1, mine] * proj[pl.ds(8 - s + start, N2), columns] for s in range(3)
        )

    for n in (1, 2, 3, 0):
        if n == 0:
            receive(("halo",), halo_in)
            before = halo_in[...].astype(F32)[8:, :]
            proj[:8, :] = jnp.where(z > 0, before, 0.0)
        values = []
        for start in (n * ROWS, n * ROWS + N2):
            rows = pl.ds(start, N2)
            query[rows, :] = short(start, 0)
            values.append(short(start, 1) * short(start, 2))
            signal[rows, :] = values[-1]
        sig_t[n] = by_channel(*values)

    for part in range(PARTS):
        across("sz", part, sig_t, x_in)
    for part in range(PARTS):
        filter_transform(part)

    for part in range(PARTS):
        across_wait("sz", part, x_in)
        transform(x_in, part)
        for c in range(CW):
            rows = pl.ds(c * N1, N1)
            a_re, a_im = stage[rows, :N2], stage[rows, N2:]
            b_re, b_im = spec_h[part, rows, :N2], spec_h[part, rows, N2:]
            in_halves(
                c, jnp.concatenate([a_re * b_re - a_im * b_im, a_re * b_im + a_im * b_re], axis=1)
            )
        stage[...] = dot(split_rows[...], second_back[...])
        turned = []
        for c in range(CW):
            rows = pl.ds(c * N1, N1)
            re, im = stage[rows, :N2], stage[rows, N2:]
            turned.append(
                jnp.concatenate(
                    [re * twiddle[0] + im * twiddle[1], im * twiddle[0] - re * twiddle[1]], axis=0
                )
            )
        top, rest = halves(jnp.concatenate(turned, axis=1))
        values = dot(first_back[...], jnp.concatenate([top, rest, top], axis=0))
        for c in range(CW):
            spread[pl.ds(c, N1, stride=CW), :] = values[:, c * N2:(c + 1) * N2]
        y_out[part] = spread[...].astype(BF).reshape(Z * Y, 2 * CW, N2)
        for d in FAR_FIRST:
            send(
                ("yz", part, d),
                y_out.at[part, pl.ds(((z + d) % Z) * Y, Y)],
                conv_t.at[:, part, z],
                device(dz=d),
            )
        conv_t[:, part, z] = y_out[part, pl.ds(z * Y, Y)]
    for part in range(PARTS):
        for d in range(1, Z):
            receive(("yz", part, d), conv_t.at[:, part, (z - d + Z) % Z])

    for d in (2, 1, 3, 0):
        to = (y + d) % Y
        conv = conv_t[to].astype(F32).reshape(PARTS * Z, 2, CW, N2)
        for i in range(2):
            rows = pl.ds(pl.multiple_of(to * ROWS + i * N2, N2), N2)
            long = conv[:, i].reshape(CH, N2).T + bias[:, mine] * signal[rows, :]
            gated[rows, :] = (query[rows, :] * long).astype(BF)
        rows = pl.ds(pl.multiple_of(to * ROWS, ROWS), ROWS)
        if d:
            send(("out", d), gated.at[rows, :], out.at[:, mine], device(dy=d))
        else:
            out[:, mine] = gated[rows, :]
    for d in range(1, Y):
        columns = pl.ds(pl.multiple_of(((y - d + Y) % Y) * CH, CH), CH)
        receive(("out", d), out.at[:, columns])
    for copy in sent:
        copy.wait_send()


COPIES = 9 + 28 + 30 + 16 + 3 + 1 + 3 * 7 * PARTS + 3


def on_device(tokens, w_in, taps, filt, bias):
    w_parts = w_in.transpose(2, 0, 1, 3)
    any_space = pl.BlockSpec(memory_space=pl.ANY)
    vmem = pl.BlockSpec(memory_space=pltpu.VMEM)
    scratch = [
        pltpu.VMEM((ROWS, Y * CH), F32),
        pltpu.VMEM((3, 3, Y * CH), F32),
        pltpu.VMEM((1, Y * CH), F32),
        *(pltpu.VMEM(t.shape, t.dtype) for t in tables()),
        pltpu.VMEM((2 * X, GROUP, FEAT), BF),
        pltpu.VMEM((Z, 2 * X, Y * WR, 3 * CH), BF),
        pltpu.VMEM((GROUP, 3 * CH), F32),
        pltpu.VMEM((GROUP + 8, 3 * CH), F32),
        pltpu.VMEM((16, 3 * CH), BF),
        pltpu.VMEM((16, 3 * CH), BF),
        pltpu.VMEM((GROUP, CH), F32),
        pltpu.VMEM((GROUP, CH), F32),
        pltpu.VMEM((Y, PARTS, Z, 2 * CW, N2), BF),
        pltpu.VMEM((Y, PARTS, Z, 2 * CW, N2), BF),
        pltpu.VMEM((GROUP, CH), BF),
        pltpu.VMEM((Y, PARTS, Z, 2 * CW, N2), BF),
        pltpu.VMEM((Y, PARTS, Z, 2 * CW, N2), BF),
        pltpu.VMEM((PARTS, Z * Y, 2 * CW, N2), BF),
        pltpu.VMEM((PARTS, Z * Y, 2 * CW, N2), BF),
        pltpu.VMEM((N1 * CW, N2), F32),
        pltpu.VMEM((CW * N1, 2 * N2), F32),
        pltpu.VMEM((CW * N1, 6 * N2), BF),
        pltpu.VMEM((PARTS, CW * N1, 2 * N2), F32),
        pltpu.VMEM((PARTS, Z * Y, 2 * CW, N2), BF),
        pltpu.SemaphoreType.DMA((COPIES,)),
        pltpu.SemaphoreType.DMA((COPIES,)),
        pltpu.SemaphoreType.DMA((12,)),
    ]
    return pl.pallas_call(
        kernel,
        out_shape=jax.ShapeDtypeStruct((ROWS, Y * CH), BF),
        in_specs=[any_space] * 10,
        out_specs=vmem,
        scratch_shapes=scratch,
        compiler_params=pltpu.CompilerParams(
            collective_id=0, has_side_effects=True, vmem_limit_bytes=60 * 1024 * 1024
        ),
        name="layer",
    )(tokens, w_parts, filt, taps, bias[None, :], *(jnp.asarray(t) for t in tables()))


def solution(mesh):
    return jax.shard_map(
        on_device,
        mesh=mesh,
        in_specs=(
            P("seq", "ch"),
            P(None, "seq", None, "ch"),
            P(None, None, "ch"),
            P("seq", "ch"),
            P("ch"),
        ),
        out_specs=P("seq", "ch"),
        check_vma=False,
    )
```

time: 138 us -> 108 us (0.78)
  Pallas kernels: 131 us -> 105 us
  local copies, waits for them, and re-layouts: 6.71 us -> 3.75 us
    pallas_call x1, Pallas kernels: 131 us -> 105 us  [on_device(): pl.pallas_call(kernel, out_shape=jax.ShapeDtypeStruct((ROWS, Y * CH), BF)...]
    reshape x3 -> x0, local copies, waits for them, and re-layouts: 5.95 us -> none  [the longest x2 3.39 us: on_device(): w_parts = w_in.reshape(2 * X, WR, 3, Y, CH).transpose(3, 0, 1, 2, 4)]
    unnamed x19 -> x2, local copies, waits for them, and re-layouts: 0.75 us -> 3.75 us
where the time goes in v2:
time: 108 us
  Pallas kernels  105 us (97%)
  local copies, waits for them, and re-layouts  3.75 us (3%)
    pallas_call x1, Pallas kernels, on_device(): pl.pallas_call(kernel, out_shape=jax.ShapeDtypeStruct((ROWS, Y * CH), BF)...  105 us
    unnamed x2, local copies, waits for them, and re-layouts  3.75 us

profile of v2, /device:TPU:2, one launch (start us, length us, event | category | flops | bytes accessed | tf_op | source)
XLA Modules:
  0.0 108.3 jit_solution(15903776419935686119)
XLA Ops:
  0.0 2.1 %copy.13 = bf16[8,32,3,512]{3,1,0,2:T(8,128)(2,1)} copy(bf16[8,32,3,512]{3,1,2,0:T(8,128)(2,1)} %param.11) | data formatting | bytes 1572864 | tf_op args[1]
  2.1 104.5 %layer.1 = bf16[256,512]{1,0:T(8,128)(2,1)} custom-call(bf16[256,1024]{1,0:T(8,128)(2,1)} %tok_in.1, bf16[3,8,32,512]{3,2,1,0:T(8,128)(2,1)} %bitcast.4, f32[256,512]{1,0:T(8,128)} %filt_in.1, f32[3,3,512]{2,1,0:T(4,128)} %taps_in.1, f32[1,512]{1,0:T(1,128)} %bitcast.5, bf16[128,128]{1,0:T(8,128)(2,1)} %constant.10.clone.first_in, ...), custom_call_target="tpu_custom_call" | custom-call | tf_op jit(solution)/shard_map/layer/pallas_call | solution.py:478
  106.6 1.7 %copy.15 = bf16[256,512]{1,0:T(8,128)(2,1)} copy(bf16[256,512]{1,0:T(8,128)(2,1)} %layer.1) | data formatting | bytes 524288

commit v3 on v2

--- a/solution.py
+++ b/solution.py
@@ -72,7 +72,7 @@
 def kernel(
     tok_in, w_in, filt_in, taps_in, bias_in, first_in, first_back_in, twiddle_in, second_in,
     second_back_in, out,
-    filt, taps, bias, first, first_back, twiddle, second, second_back, tok, wall, acc, proj, halo_out, halo_in, query, signal, sig_t, conv_t, gated,
+    filt, taps, bias, first, first_back, twiddle, second, second_back, tok, wall, acc, proj, halo_out, halo_in, share_out, share_in, sig_t, conv_in,
     filt_t, filt_z, x_in, h_in, spread, stage, split_rows, spec_h, y_out,
     send_sem, recv_sem, local_sem,
 ):
@@ -125,7 +125,7 @@
 
     own_tok = pltpu.make_async_copy(tok_in, t_place(0, 0), local_sem.at[0])
     def w_columns(to, j):
-        return w_in.at[j, :, :, pl.ds(to * CH, CH)]
+        return w_in.at[:, j, :, pl.ds(to * CH, CH)]
 
     def w_home(j):
         return wall.at[z, :, pl.ds(y * WR, WR), pl.ds(j * CH, CH)]
@@ -137,7 +137,7 @@
     for copy in own[:1] + own_w + [own_tok] + own[1:]:
         copy.start()
 
-    peers = [device(dz=d) for d in range(1, Z)] + [device(dy=d) for d in range(1, Y)]
+    peers = [device(dz=dz, dy=dy) for dz in range(Z) for dy in range(Y) if dz or dy]
     peers += [device(dx=1), device(dx=-1), device(flip=True)]
     barrier = pltpu.get_barrier_semaphore()
     for peer in peers:
@@ -146,7 +146,7 @@
     own[0].wait()
     for quarter in range(Y):
         columns = slice(quarter * CH, (quarter + 1) * CH)
-        filt_t[quarter] = by_channel(filt[:N2, columns], filt[N2:, columns])
+        filt_t[:, :, quarter] = by_channel(filt[:N2, columns], filt[N2:, columns])
     acc[...] = jnp.zeros_like(acc)
 
     pl.semaphore_wait(barrier, len(peers))
@@ -168,6 +168,9 @@
     z_send(0, 0, False)
     w_send(1)
     w_send(2)
+    for d in FAR_FIRST:
+        send(("fz", 0, d), filt_t.at[0, (z + d) % Z], filt_z.at[0, z], device(dz=d))
+    filt_z[0, z] = filt_t[0, z]
     own_tok.wait()
     for copy in own[1:]:
         copy.wait()
@@ -228,19 +231,22 @@
     begin_b(0)
     to_sibling(0, 0)
 
-    def across(name, part, src, dst):
+    def across(name, blocks, part, src, dst):
+        start, count = blocks
         for d in FAR_FIRST:
             send(
-                (name, part, d),
-                src.at[:, part, (z + d) % Z],
-                dst.at[part, pl.ds(z * Y, Y)],
+                (name, part, start, d),
+                src.at[pl.ds(start, count), part, (z + d) % Z],
+                dst.at[part, pl.ds(z * Y + start, count)],
                 device(dz=d),
             )
-        dst[part, pl.ds(z * Y, Y)] = src[:, part, z]
-
-    def across_wait(name, part, dst):
-        for d in range(1, Z):
-            receive((name, part, d), dst.at[part, pl.ds(((z - d + Z) % Z) * Y, Y)])
+        dst[part, pl.ds(z * Y + start, count)] = src[start:start + count, part, z]
+
+    def across_wait(name, blocks, part, dst):
+        start, count = blocks
+        for d in FAR_FIRST:
+            place = dst.at[part, pl.ds((z - d + Z) % Z * Y + start, count)]
+            receive((name, part, start, d), place)
 
     def transform(source, part):
         spread[...] = source[part].astype(F32).reshape(N1 * CW, N2)
@@ -264,21 +270,34 @@
         split_rows[rows, 2 * N2:4 * N2] = rest
         split_rows[rows, 4 * N2:] = top
 
-    def filter_across():
-        for d in range(1, Y):
-            receive(("fy", d), filt_z.at[(y - d + Y) % Y])
-        for part in range(PARTS):
-            across("fz", part, filt_z, h_in)
+    def filter_second():
+        for d in FAR_FIRST:
+            receive(("fz", 0, d), filt_z.at[0, (z - d + Z) % Z])
+        for d in (2, 1, 3):
+            send(("fy", 0, d), filt_z.at[0, :, (y + d) % Y], h_in.at[0, :, y], device(dy=d))
+        h_in[0, :, y] = filt_z[0, :, y]
+
+    def filter_last():
+        for d in (2, 1, 3):
+            receive(("fy", 1, d), filt_z.at[1, :, (y - d + Y) % Y])
+        for d in FAR_FIRST:
+            send(("fz", 1, d), filt_z.at[1, (z + d) % Z], h_in.at[1, z], device(dz=d))
+        h_in[1, z] = filt_z[1, z]
 
     def filter_transform(part):
-        across_wait("fz", part, h_in)
+        if part == 0:
+            for d in (2, 1, 3):
+                receive(("fy", 0, d), h_in.at[0, :, (y - d + Y) % Y])
+        else:
+            for d in FAR_FIRST:
+                receive(("fz", 1, d), h_in.at[1, (z - d + Z) % Z])
         transform(h_in, part)
         spec_h[part] = stage[...]
 
     def filter_send():
-        for d in range(1, Y):
-            send(("fy", d), filt_t.at[(y + d) % Y], filt_z.at[y], device(dy=d))
-        filt_z[y] = filt_t[y]
+        for d in (2, 1, 3):
+            send(("fy", 1, d), filt_t.at[1, :, (y + d) % Y], filt_z.at[1, :, y], device(dy=d))
+        filt_z[1, :, y] = filt_t[1, :, y]
 
     def w_next(p):
         for j in range(3):
@@ -301,48 +320,58 @@
         left, right = [], []
         for offset in offsets:
             source = (z + offset + Z) % Z
-            for b in blocks:
-                left.append(tok[b, rows, pl.ds(pl.multiple_of(source * N2, N2), N2)])
-                right.append(wall[source, b])
+            lanes = pl.ds(pl.multiple_of(source * N2, N2), N2)
+            left += [tok[b, rows, lanes] for b in blocks]
+            right += [wall[source, b] for b in blocks]
         return acc[rows, :] + dot(jnp.concatenate(left, axis=1), jnp.concatenate(right, axis=0))
+
+    def all_rows(blocks, offsets):
+        def rows_of(n, carry):
+            rows = pl.ds(pl.multiple_of(n * 2 * ROWS, 2 * ROWS), 2 * ROWS)
+            acc[rows, :] = total(blocks, rows, offsets)
+            return carry
+
+        lax.fori_loop(0, GROUP // (2 * ROWS), rows_of, 0)
 
     EARLY = (0, -1, 1, -2, 2)
     LATE = (-3, 3)
-
-    def unit(ring):
+    ODD = range(1, 2 * X, 2)
+
+    def from_sibling(ring):
         for step in (-1, 1, 2):
             dy = OFFSET[ring] * (1 - core) + step * core
             dx = OFFSET[ring] * core + step * (1 - core)
             receive(("s", ring, step), t_place(dy + Y, dx + X, other=True))
         step = OFFSET[ring]
         receive(("s", 0, step), t_place(step * (1 - core) + Y, step * core + X, other=True))
-        column = (x + OFFSET[ring] + X) % X
-
+
+    def even_early():
+        for ring in (1, 2, 3):
+            from_sibling(ring)
+        all_rows([(x + OFFSET[ring] + X) % X * 2 for ring in (1, 2, 3)], EARLY)
+
+    def odd_early():
         def rows_of(n, carry):
-            rows = pl.ds(pl.multiple_of(n * ROWS, ROWS), ROWS)
-            acc[rows, :] = total([column * 2], rows, EARLY)
+            rows = pl.ds(pl.multiple_of((y + n + Y - 1) % Y * ROWS, ROWS), ROWS)
+            acc[rows, :] = total(ODD, rows, EARLY)
             return carry
 
-        lax.fori_loop(0, Y, rows_of, 0)
-        rows = pl.ds(pl.multiple_of(((y + OFFSET[ring] + Y) % Y) * ROWS, ROWS), ROWS)
-        acc[rows, :] = total([2 * b + 1 for b in range(X)], rows, EARLY)
-
-    def late():
-        def rows_of(n, carry):
-            rows = pl.ds(pl.multiple_of(n * ROWS, ROWS), ROWS)
-            acc[rows, :] = total(range(2 * X), rows, LATE)
-            return carry
-
-        lax.fori_loop(0, Y, rows_of, 0)
+        lax.fori_loop(0, 3, rows_of, 0)
+
+    def rest():
+        from_sibling(4)
+        rows = pl.ds(pl.multiple_of((y + 2) % Y * ROWS, ROWS), ROWS)
+        acc[rows, :] = total(ODD, rows, EARLY)
+        all_rows([(x + 2) % X * 2], EARLY)
+        all_rows(range(2 * X), LATE)
 
     order = [
-        (w_next, 1), (w_next, 2), (near_first, 0), (begin, 1), (filter_send,), (w_next, 3), (z_next, 0),
+        (w_next, 1), (w_next, 2), (near_first, 0), (begin, 1), (w_next, 3), (z_next, 0),
         (near_second, 0), (begin, 2), (begin, 3), (near_first, 1), (z_next, 1), (near_second, 1), (z_next, 2),
         (z_next, 3), (near_first, 2), (far, 0), (begin, 4), (near_second, 2), (z_next, 4),
         (near_first, 3), (z_next, 5), (near_second, 3), (near_first, 4), (z_next, 6),
-        (near_second, 4), (z_next, 7), (far, 1), (far, 2), (z_next, 8), (far, 3), (z_next, 9),
-        (far, 4), (z_next, 10), (z_next, 11), (filter_across,), (unit, 1), (unit, 2), (unit, 3), (unit, 4),
-        (late,),
+        (near_second, 4), (filter_send,), (filter_second,), (z_next, 7), (far, 1), (far, 2), (z_next, 8), (far, 3), (z_next, 9),
+        (z_next, 10), (even_early,), (z_next, 11), (far, 4), (filter_last,), (odd_early,), (rest,),
     ]
     for event, *values in order:
         event(*values)
@@ -350,41 +379,56 @@
     for p in range(4):
         receive(("z", p < 2, 4, p), w_place(4, p))
 
-    for n in (3, 0, 1, 2):
+    mine = pl.ds(pl.multiple_of(y * CH, CH), CH)
+
+    def project(n):
         rounded = total(range(2 * X), pl.ds(n * ROWS, ROWS), (4,)).astype(BF)
         proj[pl.ds(8 + n * ROWS, ROWS), :] = rounded.astype(F32)
         if n == 3:
             halo_out[...] = rounded[ROWS - 16:, :]
             send(("halo",), halo_out, halo_in, device(dz=1))
 
-    mine = pl.ds(pl.multiple_of(y * CH, CH), CH)
-
     def short(start, j):
         columns = slice(j * CH, (j + 1) * CH)
         return sum(
             taps[s, j:j + 1, mine] * proj[pl.ds(8 - s + start, N2), columns] for s in range(3)
         )
 
-    for n in (1, 2, 3, 0):
-        if n == 0:
-            receive(("halo",), halo_in)
-            before = halo_in[...].astype(F32)[8:, :]
-            proj[:8, :] = jnp.where(z > 0, before, 0.0)
+    def gate(n):
         values = []
         for start in (n * ROWS, n * ROWS + N2):
-            rows = pl.ds(start, N2)
-            query[rows, :] = short(start, 0)
+            query = short(start, 0)
             values.append(short(start, 1) * short(start, 2))
-            signal[rows, :] = values[-1]
+            at = pl.ds(start - n * ROWS, N2)
+            share_out[n, 0, at, :] = query.astype(BF)
+            share_out[n, 1, at, :] = (query * (bias[:, mine] * values[-1])).astype(BF)
         sig_t[n] = by_channel(*values)
 
+    BLOCKS = ((2, 2), (0, 2))
+    project(3)
+    project(2)
+    project(1)
+    gate(3)
+    gate(2)
     for part in range(PARTS):
-        across("sz", part, sig_t, x_in)
+        across("sz", BLOCKS[0], part, sig_t, x_in)
+    project(0)
+    gate(1)
+    receive(("halo",), halo_in)
+    before = halo_in[...].astype(F32)[8:, :]
+    proj[:8, :] = jnp.where(z > 0, before, 0.0)
+    gate(0)
+    for part in range(PARTS):
+        across("sz", BLOCKS[1], part, sig_t, x_in)
+    for d in (2, 1, 3):
+        send(("share", d), share_out.at[(y + d) % Y], share_in.at[y], device(dy=d))
+    share_in[y] = share_out[y]
     for part in range(PARTS):
         filter_transform(part)
 
     for part in range(PARTS):
-        across_wait("sz", part, x_in)
+        for blocks in BLOCKS:
+            across_wait("sz", blocks, part, x_in)
         transform(x_in, part)
         for c in range(CW):
             rows = pl.ds(c * N1, N1)
@@ -408,43 +452,45 @@
         for c in range(CW):
             spread[pl.ds(c, N1, stride=CW), :] = values[:, c * N2:(c + 1) * N2]
         y_out[part] = spread[...].astype(BF).reshape(Z * Y, 2 * CW, N2)
-        for d in FAR_FIRST:
-            send(
-                ("yz", part, d),
-                y_out.at[part, pl.ds(((z + d) % Z) * Y, Y)],
-                conv_t.at[:, part, z],
-                device(dz=d),
-            )
-        conv_t[:, part, z] = y_out[part, pl.ds(z * Y, Y)]
+        for dz in (*FAR_FIRST, 0):
+            for dy in (2, 1, 3, 0):
+                if dz or dy:
+                    to = (z + dz) % Z * Y + (y + dy) % Y
+                    send(
+                        ("conv", part, dz, dy),
+                        y_out.at[part, to],
+                        conv_in.at[part, y, z],
+                        device(dz=dz, dy=dy),
+                    )
+        conv_in[part, y, z] = y_out[part, seq]
+    for d in (2, 1, 3):
+        receive(("share", d), share_in.at[(y - d + Y) % Y])
     for part in range(PARTS):
-        for d in range(1, Z):
-            receive(("yz", part, d), conv_t.at[:, part, (z - d + Z) % Z])
-
-    for d in (2, 1, 3, 0):
-        to = (y + d) % Y
-        conv = conv_t[to].astype(F32).reshape(PARTS * Z, 2, CW, N2)
+        for dz in (*FAR_FIRST, 0):
+            for dy in (2, 1, 3, 0):
+                if dz or dy:
+                    place = conv_in.at[part, (y - dy + Y) % Y, (z - dz + Z) % Z]
+                    receive(("conv", part, dz, dy), place)
+
+    for quarter in range(Y):
+        conv = conv_in[:, quarter].astype(F32).reshape(PARTS * Z, 2, CW, N2)
+        columns = slice(quarter * CH, (quarter + 1) * CH)
         for i in range(2):
-            rows = pl.ds(pl.multiple_of(to * ROWS + i * N2, N2), N2)
-            long = conv[:, i].reshape(CH, N2).T + bias[:, mine] * signal[rows, :]
-            gated[rows, :] = (query[rows, :] * long).astype(BF)
-        rows = pl.ds(pl.multiple_of(to * ROWS, ROWS), ROWS)
-        if d:
-            send(("out", d), gated.at[rows, :], out.at[:, mine], device(dy=d))
-        else:
-            out[:, mine] = gated[rows, :]
-    for d in range(1, Y):
-        columns = pl.ds(pl.multiple_of(((y - d + Y) % Y) * CH, CH), CH)
-        receive(("out", d), out.at[:, columns])
+            rows = slice(i * N2, (i + 1) * N2)
+            factor = share_in[quarter, 0, rows, :].astype(F32)
+            added = share_in[quarter, 1, rows, :].astype(F32)
+            out[rows, columns] = (factor * conv[:, i].reshape(CH, N2).T + added).astype(BF)
+    assert len(numbers) == COPIES
     for copy in sent:
         copy.wait_send()
 
 
-COPIES = 9 + 28 + 30 + 16 + 3 + 1 + 3 * 7 * PARTS + 3
+COPIES = 9 + 28 + 30 + 16 + 1 + (3 * 7 + 31 + 3) * PARTS + 3
 
 
 def on_device(tokens, w_in, taps, filt, bias):
-    w_parts = w_in.transpose(2, 0, 1, 3)
-    any_space = pl.BlockSpec(memory_space=pl.ANY)
+    w_parts = w_in.transpose(0, 2, 1, 3)
+    hbm = pl.BlockSpec(memory_space=pltpu.HBM)
     vmem = pl.BlockSpec(memory_space=pltpu.VMEM)
     scratch = [
         pltpu.VMEM((ROWS, Y * CH), F32),
@@ -457,15 +503,14 @@
         pltpu.VMEM((GROUP + 8, 3 * CH), F32),
         pltpu.VMEM((16, 3 * CH), BF),
         pltpu.VMEM((16, 3 * CH), BF),
-        pltpu.VMEM((GROUP, CH), F32),
-        pltpu.VMEM((GROUP, CH), F32),
+        pltpu.VMEM((Y, 2, ROWS, CH), BF),
+        pltpu.VMEM((Y, 2, ROWS, CH), BF),
         pltpu.VMEM((Y, PARTS, Z, 2 * CW, N2), BF),
-        pltpu.VMEM((Y, PARTS, Z, 2 * CW, N2), BF),
-        pltpu.VMEM((GROUP, CH), BF),
-        pltpu.VMEM((Y, PARTS, Z, 2 * CW, N2), BF),
-        pltpu.VMEM((Y, PARTS, Z, 2 * CW, N2), BF),
+        pltpu.VMEM((PARTS, Y, Z, 2 * CW, N2), BF),
+        pltpu.VMEM((PARTS, Z, Y, 2 * CW, N2), BF),
+        pltpu.VMEM((PARTS, Z, Y, 2 * CW, N2), BF),
         pltpu.VMEM((PARTS, Z * Y, 2 * CW, N2), BF),
-        pltpu.VMEM((PARTS, Z * Y, 2 * CW, N2), BF),
+        pltpu.VMEM((PARTS, Z, Y, 2 * CW, N2), BF),
         pltpu.VMEM((N1 * CW, N2), F32),
         pltpu.VMEM((CW * N1, 2 * N2), F32),
         pltpu.VMEM((CW * N1, 6 * N2), BF),
@@ -478,7 +523,7 @@
     return pl.pallas_call(
         kernel,
         out_shape=jax.ShapeDtypeStruct((ROWS, Y * CH), BF),
-        in_specs=[any_space] * 10,
+        in_specs=[hbm] * 10,
         out_specs=vmem,
         scratch_shapes=scratch,
         compiler_params=pltpu.CompilerParams(

time: 108 us -> 98.7 us (0.914)
  Pallas kernels: 105 us -> 96.9 us
  local copies, waits for them, and re-layouts: 3.75 us -> 1.67 us
    pallas_call x1, Pallas kernels: 105 us -> 96.9 us  [on_device(): pl.pallas_call(kernel, out_shape=jax.ShapeDtypeStruct((ROWS, Y * CH), BF)...]
    unnamed x2 -> x1, local copies, waits for them, and re-layouts: 3.75 us -> 1.67 us
where the time goes in v3:
time: 98.7 us; the launch traced here: 98.6 us
  Pallas kernels  96.9 us (98%)
  local copies, waits for them, and re-layouts  1.67 us (2%)
    pallas_call x1, Pallas kernels, on_device(): pl.pallas_call(kernel, out_shape=jax.ShapeDtypeStruct((ROWS, Y * CH), BF)...  96.9 us

profile of v3, /device:TPU:2, one launch (start us, length us, event | category | flops | bytes accessed | tf_op | source)
XLA Modules:
  0.0 98.6 jit_solution(13743910919969991031)
XLA Ops:
  0.0 96.9 %layer.1 = bf16[256,512]{1,0:T(8,128)(2,1)} custom-call(bf16[256,1024]{1,0:T(8,128)(2,1)} %tok_in.1, bf16[8,3,32,512]{3,2,1,0:T(8,128)(2,1)} %bitcast.2, f32[256,512]{1,0:T(8,128)} %filt_in.1, f32[3,3,512]{2,1,0:T(4,128)} %taps_in.1, f32[1,512]{1,0:T(1,128)} %bitcast.3, bf16[128,128]{1,0:T(8,128)(2,1)} %constant.10.clone.first_in, ...), custom_call_target="tpu_custom_call" | custom-call | tf_op jit(solution)/shard_map/layer/pallas_call | solution.py:523
  96.9 1.7 %copy.12 = bf16[256,512]{1,0:T(8,128)(2,1)} copy(bf16[256,512]{1,0:T(8,128)(2,1)} %layer.1) | data formatting | bytes 524288

commit v4 on v3

--- a/solution.py
+++ b/solution.py
@@ -102,6 +102,11 @@
         copy.start()
         sent.append(copy)
 
+    def sent_all(count=None):
+        for copy in sent[:count]:
+            copy.wait_send()
+        del sent[:count]
+
     def receive(key, dst):
         remote(key, dst, dst, device(flip=True)).wait_recv()
 
@@ -123,6 +128,12 @@
         dy, dx = along(axis, step)
         return device(dy=dy, dx=dx)
 
+    peers = [device(dz=dz, dy=dy) for dz in range(Z) for dy in range(Y) if dz or dy]
+    peers += [device(dx=1), device(dx=-1), device(flip=True)]
+    barrier = pltpu.get_barrier_semaphore()
+    for peer in peers:
+        pl.semaphore_signal(barrier, inc=1, device_id=peer, device_id_type=MESH)
+
     own_tok = pltpu.make_async_copy(tok_in, t_place(0, 0), local_sem.at[0])
     def w_columns(to, j):
         return w_in.at[:, j, :, pl.ds(to * CH, CH)]
@@ -136,12 +147,6 @@
     own = [pltpu.make_async_copy(a, b, local_sem.at[4 + n]) for n, (a, b) in enumerate(pairs)]
     for copy in own[:1] + own_w + [own_tok] + own[1:]:
         copy.start()
-
-    peers = [device(dz=dz, dy=dy) for dz in range(Z) for dy in range(Y) if dz or dy]
-    peers += [device(dx=1), device(dx=-1), device(flip=True)]
-    barrier = pltpu.get_barrier_semaphore()
-    for peer in peers:
-        pl.semaphore_signal(barrier, inc=1, device_id=peer, device_id_type=MESH)
 
     own[0].wait()
     for quarter in range(Y):
@@ -380,6 +385,8 @@
         receive(("z", p < 2, 4, p), w_place(4, p))
 
     mine = pl.ds(pl.multiple_of(y * CH, CH), CH)
+
+    ring_copies = len(sent)
 
     def project(n):
         rounded = total(range(2 * X), pl.ds(n * ROWS, ROWS), (4,)).astype(BF)
@@ -425,6 +432,7 @@
     share_in[y] = share_out[y]
     for part in range(PARTS):
         filter_transform(part)
+    sent_all(ring_copies)
 
     for part in range(PARTS):
         for blocks in BLOCKS:
@@ -463,6 +471,7 @@
                         device(dz=dz, dy=dy),
                     )
         conv_in[part, y, z] = y_out[part, seq]
+    sent_all()
     for d in (2, 1, 3):
         receive(("share", d), share_in.at[(y - d + Y) % Y])
     for part in range(PARTS):
@@ -481,8 +490,6 @@
             added = share_in[quarter, 1, rows, :].astype(F32)
             out[rows, columns] = (factor * conv[:, i].reshape(CH, N2).T + added).astype(BF)
     assert len(numbers) == COPIES
-    for copy in sent:
-        copy.wait_send()
 
 
 COPIES = 9 + 28 + 30 + 16 + 1 + (3 * 7 + 31 + 3) * PARTS + 3

time: 98.7 us -> 98.3 us (level)
  no operation moved by 1% of the time
where the time goes in v4:
time: 98.3 us; the launch traced here: 98.2 us
  Pallas kernels  96.5 us (98%)
  local copies, waits for them, and re-layouts  1.67 us (2%)
    pallas_call x1, Pallas kernels, on_device(): pl.pallas_call(kernel, out_shape=jax.ShapeDtypeStruct((ROWS, Y * CH), BF)...  96.5 us

profile of v4, /device:TPU:2, one launch (start us, length us, event | category | flops | bytes accessed | tf_op | source)
XLA Modules:
  0.0 98.2 jit_solution(3552454763587951322)
XLA Ops:
  0.0 96.5 %layer.1 = bf16[256,512]{1,0:T(8,128)(2,1)} custom-call(bf16[256,1024]{1,0:T(8,128)(2,1)} %tok_in.1, bf16[8,3,32,512]{3,2,1,0:T(8,128)(2,1)} %bitcast.2, f32[256,512]{1,0:T(8,128)} %filt_in.1, f32[3,3,512]{2,1,0:T(4,128)} %taps_in.1, f32[1,512]{1,0:T(1,128)} %bitcast.3, bf16[128,128]{1,0:T(8,128)(2,1)} %constant.10.clone.first_in, ...), custom_call_target="tpu_custom_call" | custom-call | tf_op jit(solution)/shard_map/layer/pallas_call | solution.py:530
  96.5 1.7 %copy.12 = bf16[256,512]{1,0:T(8,128)(2,1)} copy(bf16[256,512]{1,0:T(8,128)(2,1)} %layer.1) | data formatting | bytes 524288
